TPU v7x, 32 devices: a whole 2x2x4 slice. The times are simulated.
32 devices in a mesh: wide: 16 (over z, x, core), row: 2 (over y).
Axes of the slice: x: 2, y: 2, z: 4, core: 2. Of those that a mesh axis runs over, the one named last changes fastest.
Arguments:
- points: float32 [128, 4096], P(None, ('wide', 'row')), may hold values from -6 to 6
- targets: float32 [32, 4096], P(None, ('wide', 'row')), may hold values from -6 to 6
- lengthscales: float32 [128], replicated, may hold values from 3.5 to 7
- outputscale: float32 [1], replicated, may hold values from 0.5 to 2
- noise: float32 [1], replicated, may hold values from 0.5 to 2
Outputs:
- solution: float32 [32, 4096], P(None, ('wide', 'row'))
- residual: float32 [32, 4096], P(None, ('wide', 'row'))
All inputs are finite; a program needn't handle non-finite values.
Results may differ from a plain program's by a relative error of at most 0.0003.
Values sent between devices are 32-bit elements; how exact they have to be, the bound alone decides.
A program may use at most 64 MiB of HBM per device.

v0:
```python
import jax
import jax.numpy as jnp
from jax import lax
from jax.sharding import PartitionSpec as P

ITERS = 2


def from_behind(value, axis, steps):
    count = lax.axis_size(axis)
    pairs = [(source, (source + steps) % count) for source in range(count)]
    return lax.ppermute(value, axis, pairs)


def kernel_tile(left_pts, left_sq, right_pts, right_sq, kern_scale):
    cross = lax.dot_general(
        left_pts, right_pts, (((0,), (0,)), ((), ())), precision=lax.Precision.HIGHEST
    )
    distance = left_sq[:, None] + right_sq[None, :] - 2.0 * cross
    return kern_scale * jnp.exp(-0.5 * distance)


def apply_rows(vectors, kernel):
    return lax.dot_general(
        vectors, kernel, (((1,), (1,)), ((), ())), precision=lax.Precision.HIGHEST
    )


def apply_columns(vectors, kernel):
    return lax.dot_general(
        vectors, kernel, (((1,), (0,)), ((), ())), precision=lax.Precision.HIGHEST
    )


def on_device(points, targets, lengthscales, outputscale, noise):
    wide_count = lax.axis_size("wide")
    row_count = lax.axis_size("row")
    half_cycle = wide_count // 2
    slot_count = half_cycle // row_count
    member = lax.axis_index("row")
    scaled = points / lengthscales[:, None]
    kern_scale = outputscale[0]
    noise_var = noise[0]
    features = scaled.shape[0]
    local_count = points.shape[1]

    def collect(stacked):
        window = stacked[None]
        while window.shape[0] < half_cycle:
            arrived = from_behind(window, "wide", -window.shape[0])
            window = jnp.concatenate([window, arrived], axis=0)
        return window

    def assemble(stacked):
        across = from_behind(stacked, "wide", -half_cycle)
        table = collect(stacked)
        channels = table.shape[1]
        nearer = table.reshape(slot_count, row_count, channels, local_count).transpose(0, 2, 1, 3)
        own_block = jnp.broadcast_to(
            table[0][None, :, None, :], (1, channels, row_count, local_count)
        )
        outgoing = jnp.concatenate([own_block, nearer], axis=0)
        arrived = lax.all_to_all(outgoing, "row", split_axis=2, concat_axis=2, tiled=True)
        return (arrived.reshape(slot_count + 1, channels, row_count * local_count), across)

    solution = jnp.zeros_like(targets)
    residual = targets
    direction = targets
    norm_now = lax.psum(jnp.sum(residual * residual, axis=1), ("wide", "row"))
    cache = None
    for iteration in range(ITERS):
        operate_cache = cache
        if operate_cache is None:
            blocks, operate_across = assemble(jnp.concatenate([scaled, direction], axis=0))
            point_blocks = blocks[:, :features]
            vector_blocks = blocks[:, features:]
            far_points = operate_across[:features]
            far_vector = operate_across[features:]
            operate_cache = (
                point_blocks,
                jnp.sum(point_blocks * point_blocks, axis=1),
                far_points,
                jnp.sum(far_points * far_points, axis=0),
            )
        else:
            vector_blocks, far_vector = assemble(direction)
        point_blocks, block_sq, far_points, far_sq = operate_cache
        left_pts = point_blocks[0]
        left_sq = block_sq[0]
        left_vec = vector_blocks[0]
        kernel = kernel_tile(left_pts, left_sq, far_points, far_sq, kern_scale)
        own_rows = apply_rows(far_vector, kernel)
        operate_partials = []
        for slot_index in range(slot_count):
            kernel = kernel_tile(
                left_pts,
                left_sq,
                point_blocks[slot_index + 1],
                block_sq[slot_index + 1],
                kern_scale,
            )
            own_rows = own_rows + apply_rows(vector_blocks[slot_index + 1], kernel)
            weight = (member + row_count * slot_index != 0).astype(jnp.float32)
            operate_partials.append(weight * apply_columns(left_vec, kernel))
        partials = jnp.stack([own_rows] + operate_partials, axis=0)
        rhs_count = partials.shape[1]
        pieces = partials.reshape(slot_count + 1, rhs_count, row_count, local_count)
        spread_arrived = lax.all_to_all(pieces, "row", split_axis=2, concat_axis=2, tiled=True)
        mine = jnp.sum(spread_arrived[0], axis=1)
        by_distance = (
            spread_arrived[1:].transpose(0, 2, 1, 3).reshape(half_cycle, rhs_count, local_count)
        )
        by_distance = by_distance.at[0].add(mine)
        held = by_distance
        span_size = half_cycle
        while span_size > 1:
            span_size = span_size // 2
            held = held[:span_size] + from_behind(held[span_size:], "wide", span_size)
        summed = held[0]
        image = summed + noise_var * direction
        cache = operate_cache
        curve, cross_term, image_sq = lax.psum(
            (
                jnp.sum(direction * image, axis=1),
                jnp.sum(residual * image, axis=1),
                jnp.sum(image * image, axis=1),
            ),
            ("wide", "row"),
        )
        step_size = norm_now / curve
        norm_next = norm_now - 2.0 * step_size * cross_term + step_size * step_size * image_sq
        solution = solution + step_size[:, None] * direction
        residual = residual - step_size[:, None] * image
        if iteration + 1 < ITERS:
            direction = residual + (norm_next / norm_now)[:, None] * direction
            norm_now = norm_next
    return (solution, residual)


def solution(mesh):
    return jax.shard_map(
        on_device,
        mesh=mesh,
        in_specs=(P(None, ("wide", "row")), P(None, ("wide", "row")), P(), P(), P()),
        out_specs=(P(None, ("wide", "row")), P(None, ("wide", "row"))),
        check_vma=False,
    )
```

profile of v0, /device:TPU:0, one launch (start us, length us, event | category | flops | bytes accessed | tf_op | source)
XLA Modules:
  0.0 196.9 jit_solution(15390943010690558631)
XLA Ops:
  0.6 0.9 broadcast_divide_fusion
  1.6 5.5 %collective-permute-start.1 = (f32[1,160,128]{2,1,0:T(8,128)S(1)}, f32[1,160,128]{2,1,0:T(8,128)S(1)}, u32[]{:S(2)}, u32[]{:S(2)}) collective-permute-start(f32[1,160,128]{2,1,0:T(8,128)S(1)} %get-tuple-element.42), channel_id=1, source_target_pairs={{0,30},{2,0},{4,2},{6,4},{8,6},{10,8},{12,10},{14,12},{16,14},{18,... | collective-permute-start | bytes 245768 | tf_op jit(solution)/shard_map/ppermute | solution.py:12
  7.1 2.1 %collective-permute-done.1 = f32[1,160,128]{2,1,0:T(8,128)S(1)} collective-permute-done((f32[1,160,128]{2,1,0:T(8,128)S(1)}, f32[1,160,128]{2,1,0:T(8,128)S(1)}, u32[]{:S(2)}, u32[]{:S(2)}) %collective-permute-start.1) | collective-permute-done | bytes 81952 | tf_op jit(solution)/shard_map/ppermute | solution.py:12
  9.2 0.6 collective-permute-start.2
  9.8 4.8 %collective-permute-done.2 = f32[2,160,128]{2,1,0:T(8,128)S(1)} collective-permute-done((f32[2,160,128]{2,1,0:T(8,128)S(1)}, f32[2,160,128]{2,1,0:T(8,128)S(1)}, u32[]{:S(2)}, u32[]{:S(2)}) %collective-permute-start.2) | collective-permute-done | bytes 163872 | tf_op jit(solution)/shard_map/ppermute | solution.py:12
  14.6 0.5 collective-permute-start.3
  15.1 9.6 %collective-permute-done.3 = f32[4,160,128]{2,1,0:T(8,128)S(1)} collective-permute-done((f32[4,160,128]{2,1,0:T(8,128)S(1)}, f32[4,160,128]{2,1,0:T(8,128)S(1)}, u32[]{:S(2)}, u32[]{:S(2)}) %collective-permute-start.3) | collective-permute-done | bytes 327712 | tf_op jit(solution)/shard_map/ppermute | solution.py:12
  24.8 0.9 copy.29
  25.7 3.5 %all-to-all-start = ((f32[5,160,2,128]{3,1,0,2:T(8,128)}), f32[5,160,2,128]{3,1,0,2:T(8,128)S(1)}, u32[]{:S(2)}, u32[]{:S(2)}) async-start(f32[5,160,2,128]{3,1,0,2:T(8,128)} %copy.29), calls=%async_computation | async-start | bytes 1638400 | tf_op jit(solution)/shard_map/all_to_all | solution.py:63
  29.3 1.0 collective-permute-start
  31.0 5.4 %collective-permute-done = f32[160,128]{1,0:T(8,128)S(1)} collective-permute-done((f32[160,128]{1,0:T(8,128)S(1)}, f32[160,128]{1,0:T(8,128)S(1)}, u32[]{:S(2)}, u32[]{:S(2)}) %collective-permute-start) | collective-permute-done | bytes 81952 | tf_op jit(solution)/shard_map/ppermute | solution.py:12
  36.4 4.9 %all-to-all-done = f32[5,160,2,128]{3,1,0,2:T(8,128)S(1)} async-done(((f32[5,160,2,128]{3,1,0,2:T(8,128)}), f32[5,160,2,128]{3,1,0,2:T(8,128)S(1)}, u32[]{:S(2)}, u32[]{:S(2)}) %all-to-all-start) | async-done | bytes 819232 | tf_op jit(solution)/shard_map/all_to_all | solution.py:63
  41.2 0.1 copy_bitcast_fusion
  41.3 0.1 fusion.18
  41.3 0.4 fusion.13
  41.8 0.3 fusion.34
  42.1 0.2 convolution_multiply_fusion.11
  42.4 0.4 fusion.12
  42.9 0.3 fusion.35
  43.2 0.2 convolution_multiply_fusion.12
  43.5 0.4 fusion.14
  43.9 0.4 exponential_multiply_fusion
  44.3 0.2 fusion.17
  44.6 0.3 convolution_add_fusion.4
  44.9 0.2 convolution_multiply_fusion.10
  45.2 0.4 fusion.15
  45.7 0.3 convolution_add_fusion.3
  46.0 0.2 convolution_multiply_fusion.9
  46.4 7.0 %all_to_all.20 = f32[5,32,2,128]{3,1,0,2:T(8,128)S(1)} all-to-all(f32[5,32,2,128]{3,1,0,2:T(8,128)S(1)} %copy_dynamic-update-slice_fusion.5), channel_id=1, replica_groups=mesh['wide'=16,'row'=2] {'row'}, dimensions={2} | all-to-all | bytes 327680 | tf_op jit(solution)/shard_map/all_to_all | solution.py:108
  53.5 6.0 %collective-permute-done.4 = f32[4,32,128]{2,1,0:T(8,128)S(1)} collective-permute-done((f32[4,32,128]{2,1,0:T(8,128)S(1)}, f32[4,32,128]{2,1,0:T(8,128)S(1)}, u32[]{:S(2)}, u32[]{:S(2)}) %collective-permute-start.4) | collective-permute-done | bytes 65568 | tf_op jit(solution)/shard_map/ppermute | solution.py:12
  59.6 0.6 collective-permute-start.5
  60.2 6.1 %collective-permute-done.5 = f32[2,32,128]{2,1,0:T(8,128)S(1)} collective-permute-done((f32[2,32,128]{2,1,0:T(8,128)S(1)}, f32[2,32,128]{2,1,0:T(8,128)S(1)}, u32[]{:S(2)}, u32[]{:S(2)}) %collective-permute-start.5) | collective-permute-done | bytes 32800 | tf_op jit(solution)/shard_map/ppermute | solution.py:12
  67.0 5.2 %collective-permute-done.6 = f32[1,32,128]{2,1,0:T(8,128)S(1)} collective-permute-done((f32[1,32,128]{2,1,0:T(8,128)S(1)}, f32[1,32,128]{2,1,0:T(8,128)S(1)}, u32[]{:S(2)}, u32[]{:S(2)}) %collective-permute-start.6) | collective-permute-done | bytes 16416 | tf_op jit(solution)/shard_map/ppermute | solution.py:12
  72.2 0.1 multiply_reduce_fusion.3
  72.3 36.9 %all-reduce = (f32[32]{0:T(128)S(1)}, f32[32]{0:T(128)S(1)}, f32[32]{0:T(128)S(1)}) all-reduce(f32[32]{0:T(128)S(1)} %get-tuple-element.27, f32[32]{0:T(128)S(1)} %get-tuple-element.28, f32[32]{0:T(128)S(1)} %get-tuple-element.26), channel_id=1, replica_groups=mesh['wide'=16,'row'=2] {'wide','row'}, use_global_device_ids=true, to_apply=%region_8.0 | all-reduce | flops 96 | bytes 768 | tf_op jit(solution)/shard_map/psum | solution.py:122
  109.3 0.1 multiply_add_fusion.1
  109.3 1.2 collective-permute-start.8
  110.5 1.4 collective-permute-done.8
  112.0 2.8 %collective-permute-start.9 = (f32[2,32,128]{2,1,0:T(8,128)S(1)}, f32[2,32,128]{2,1,0:T(8,128)S(1)}, u32[]{:S(2)}, u32[]{:S(2)}) collective-permute-start(f32[2,32,128]{2,1,0:T(8,128)S(1)} %pad_maximum_fusion.8), channel_id=1, source_target_pairs={{0,28},{2,30},{4,0},{6,2},{8,4},{10,6},{12,8},{14,10},{16,12},{18,... | collective-permute-start | bytes 98312 | tf_op jit(solution)/shard_map/ppermute | solution.py:12
  114.8 1.6 collective-permute-done.9
  116.4 2.1 %collective-permute-start.10 = (f32[4,32,128]{2,1,0:T(8,128)S(1)}, f32[4,32,128]{2,1,0:T(8,128)S(1)}, u32[]{:S(2)}, u32[]{:S(2)}) collective-permute-start(f32[4,32,128]{2,1,0:T(8,128)S(1)} %pad_maximum_fusion.7), channel_id=1, source_target_pairs={{0,24},{2,26},{4,28},{6,30},{8,0},{10,2},{12,4},{14,6},{16,8},{18,... | collective-permute-start | bytes 196616 | tf_op jit(solution)/shard_map/ppermute | solution.py:12
  118.5 2.7 %collective-permute-done.10 = f32[4,32,128]{2,1,0:T(8,128)S(1)} collective-permute-done((f32[4,32,128]{2,1,0:T(8,128)S(1)}, f32[4,32,128]{2,1,0:T(8,128)S(1)}, u32[]{:S(2)}, u32[]{:S(2)}) %collective-permute-start.10) | collective-permute-done | bytes 65568 | tf_op jit(solution)/shard_map/ppermute | solution.py:12
  121.2 0.7 copy.37
  121.9 3.4 %all-to-all-start.2 = ((f32[5,32,2,128]{3,1,0,2:T(8,128)}), f32[5,32,2,128]{3,1,0,2:T(8,128)S(1)}, u32[]{:S(2)}, u32[]{:S(2)}) async-start(f32[5,32,2,128]{3,1,0,2:T(8,128)} %copy.37), calls=%async_computation.2 | async-start | bytes 327680 | tf_op jit(solution)/shard_map/all_to_all | solution.py:63
  125.3 1.8 collective-permute-start.7
  127.1 2.9 %all-to-all-done.2 = f32[5,32,2,128]{3,1,0,2:T(8,128)S(1)} async-done(((f32[5,32,2,128]{3,1,0,2:T(8,128)}), f32[5,32,2,128]{3,1,0,2:T(8,128)S(1)}, u32[]{:S(2)}, u32[]{:S(2)}) %all-to-all-start.2) | async-done | bytes 163872 | tf_op jit(solution)/shard_map/all_to_all | solution.py:63
  130.0 0.2 convolution_multiply_fusion.5
  130.3 0.2 convolution_multiply_fusion.6
  130.5 0.2 convolution_multiply_fusion.7
  130.8 0.2 convolution_multiply_fusion.8
  131.0 0.3 fusion.28
  131.4 0.3 fusion.31
  132.0 0.2 fusion.16
  132.2 0.3 convolution_add_fusion.1
  132.6 0.3 convolution_add_fusion
  133.0 7.0 %all_to_all.21 = f32[5,32,2,128]{3,1,0,2:T(8,128)S(1)} all-to-all(f32[5,32,2,128]{3,1,0,2:T(8,128)S(1)} %copy_dynamic-update-slice_fusion), channel_id=1, replica_groups=mesh['wide'=16,'row'=2] {'row'}, dimensions={2} | all-to-all | bytes 327680 | tf_op jit(solution)/shard_map/all_to_all | solution.py:108
  140.1 1.7 collective-permute-start.11
  141.7 4.5 %collective-permute-done.11 = f32[4,32,128]{2,1,0:T(8,128)S(1)} collective-permute-done((f32[4,32,128]{2,1,0:T(8,128)S(1)}, f32[4,32,128]{2,1,0:T(8,128)S(1)}, u32[]{:S(2)}, u32[]{:S(2)}) %collective-permute-start.11) | collective-permute-done | bytes 65568 | tf_op jit(solution)/shard_map/ppermute | solution.py:12
  146.2 4.0 %collective-permute-start.12 = (f32[2,32,128]{2,1,0:T(8,128)S(1)}, f32[2,32,128]{2,1,0:T(8,128)S(1)}, u32[]{:S(2)}, u32[]{:S(2)}) collective-permute-start(f32[2,32,128]{2,1,0:T(8,128)S(1)} %slice.266), channel_id=1, source_target_pairs={{0,4},{2,6},{4,8},{6,10},{8,12},{10,14},{12,16},{14,18},{16,20},{1... | collective-permute-start | bytes 98312 | tf_op jit(solution)/shard_map/ppermute | solution.py:12
  150.2 3.0 %collective-permute-done.12 = f32[2,32,128]{2,1,0:T(8,128)S(1)} collective-permute-done((f32[2,32,128]{2,1,0:T(8,128)S(1)}, f32[2,32,128]{2,1,0:T(8,128)S(1)}, u32[]{:S(2)}, u32[]{:S(2)}) %collective-permute-start.12) | collective-permute-done | bytes 32800 | tf_op jit(solution)/shard_map/ppermute | solution.py:12
  153.3 5.8 %collective-permute-done.13 = f32[1,32,128]{2,1,0:T(8,128)S(1)} collective-permute-done((f32[1,32,128]{2,1,0:T(8,128)S(1)}, f32[1,32,128]{2,1,0:T(8,128)S(1)}, u32[]{:S(2)}, u32[]{:S(2)}) %collective-permute-start.13) | collective-permute-done | bytes 16416 | tf_op jit(solution)/shard_map/ppermute | solution.py:12
  159.2 0.1 multiply_reduce_fusion.1
  159.3 36.9 %psum.34 = f32[32]{0:T(128)S(1)} all-reduce(f32[32]{0:T(128)S(1)} %multiply_reduce_fusion.1), channel_id=1, replica_groups=mesh['wide'=16,'row'=2] {'wide','row'}, use_global_device_ids=true, to_apply=%region_11.0 | all-reduce | flops 32 | bytes 256 | tf_op jit(solution)/shard_map/psum | solution.py:122
  196.2 0.7 multiply_subtract_fusion
  (65 shorter events, 1.0 us)
Async XLA Ops:
  0.6 1.0 copy-start
  1.6 7.5 %collective-permute-start.1 = (f32[1,160,128]{2,1,0:T(8,128)S(1)}, f32[1,160,128]{2,1,0:T(8,128)S(1)}, u32[]{:S(2)}, u32[]{:S(2)}) collective-permute-start(f32[1,160,128]{2,1,0:T(8,128)S(1)} %get-tuple-element.42), channel_id=1, source_target_pairs={{0,30},{2,0},{4,2},{6,4},{8,6},{10,8},{12,10},{14,12},{16,14},{18,... | collective-permute-start | bytes 245768 | tf_op jit(solution)/shard_map/ppermute | solution.py:12
  9.2 5.4 %collective-permute-start.2 = (f32[2,160,128]{2,1,0:T(8,128)S(1)}, f32[2,160,128]{2,1,0:T(8,128)S(1)}, u32[]{:S(2)}, u32[]{:S(2)}) collective-permute-start(f32[2,160,128]{2,1,0:T(8,128)S(1)} %pad_maximum_fusion.3), channel_id=1, source_target_pairs={{0,28},{2,30},{4,0},{6,2},{8,4},{10,6},{12,8},{14,10},{16,12},{18,... | collective-permute-start | bytes 491528 | tf_op jit(solution)/shard_map/ppermute | solution.py:12
  14.6 10.1 %collective-permute-start.3 = (f32[4,160,128]{2,1,0:T(8,128)S(1)}, f32[4,160,128]{2,1,0:T(8,128)S(1)}, u32[]{:S(2)}, u32[]{:S(2)}) collective-permute-start(f32[4,160,128]{2,1,0:T(8,128)S(1)} %pad_maximum_fusion.2), channel_id=1, source_target_pairs={{0,24},{2,26},{4,28},{6,30},{8,0},{10,2},{12,4},{14,6},{16,8},{18,... | collective-permute-start | bytes 983048 | tf_op jit(solution)/shard_map/ppermute | solution.py:12
  25.7 15.5 %all-to-all-start = ((f32[5,160,2,128]{3,1,0,2:T(8,128)}), f32[5,160,2,128]{3,1,0,2:T(8,128)S(1)}, u32[]{:S(2)}, u32[]{:S(2)}) async-start(f32[5,160,2,128]{3,1,0,2:T(8,128)} %copy.29), calls=%async_computation | async-start | bytes 1638400 | tf_op jit(solution)/shard_map/all_to_all | solution.py:63
  29.3 7.0 %collective-permute-start = (f32[160,128]{1,0:T(8,128)S(1)}, f32[160,128]{1,0:T(8,128)S(1)}, u32[]{:S(2)}, u32[]{:S(2)}) collective-permute-start(f32[160,128]{1,0:T(8,128)S(1)} %get-tuple-element.41), channel_id=1, source_target_pairs={{0,16},{2,18},{4,20},{6,22},{8,24},{10,26},{12,28},{14,30},{16,0},... | collective-permute-start | bytes 245768 | tf_op jit(solution)/shard_map/ppermute | solution.py:12
  53.5 6.1 %collective-permute-start.4 = (f32[4,32,128]{2,1,0:T(8,128)S(1)}, f32[4,32,128]{2,1,0:T(8,128)S(1)}, u32[]{:S(2)}, u32[]{:S(2)}) collective-permute-start(f32[4,32,128]{2,1,0:T(8,128)S(1)} %slice.250), channel_id=1, source_target_pairs={{0,8},{2,10},{4,12},{6,14},{8,16},{10,18},{12,20},{14,22},{16,24},... | collective-permute-start | bytes 196616 | tf_op jit(solution)/shard_map/ppermute | solution.py:12
  59.6 6.7 %collective-permute-start.5 = (f32[2,32,128]{2,1,0:T(8,128)S(1)}, f32[2,32,128]{2,1,0:T(8,128)S(1)}, u32[]{:S(2)}, u32[]{:S(2)}) collective-permute-start(f32[2,32,128]{2,1,0:T(8,128)S(1)} %slice.252), channel_id=1, source_target_pairs={{0,4},{2,6},{4,8},{6,10},{8,12},{10,14},{12,16},{14,18},{16,20},{1... | collective-permute-start | bytes 98312 | tf_op jit(solution)/shard_map/ppermute | solution.py:12
  66.3 5.9 %collective-permute-start.6 = (f32[1,32,128]{2,1,0:T(8,128)S(1)}, f32[1,32,128]{2,1,0:T(8,128)S(1)}, u32[]{:S(2)}, u32[]{:S(2)}) collective-permute-start(f32[1,32,128]{2,1,0:T(8,128)S(1)} %slice.254), channel_id=1, source_target_pairs={{0,2},{2,4},{4,6},{6,8},{8,10},{10,12},{12,14},{14,16},{16,18},{18... | collective-permute-start | bytes 49160 | tf_op jit(solution)/shard_map/ppermute | solution.py:12
  109.3 2.6 %collective-permute-start.8 = (f32[1,32,128]{2,1,0:T(8,128)S(1)}, f32[1,32,128]{2,1,0:T(8,128)S(1)}, u32[]{:S(2)}, u32[]{:S(2)}) collective-permute-start(f32[1,32,128]{2,1,0:T(8,128)S(1)} %bitcast.146), channel_id=1, source_target_pairs={{0,30},{2,0},{4,2},{6,4},{8,6},{10,8},{12,10},{14,12},{16,14},{18,... | collective-permute-start | bytes 49160 | tf_op jit(solution)/shard_map/ppermute | solution.py:12
  112.0 4.4 %collective-permute-start.9 = (f32[2,32,128]{2,1,0:T(8,128)S(1)}, f32[2,32,128]{2,1,0:T(8,128)S(1)}, u32[]{:S(2)}, u32[]{:S(2)}) collective-permute-start(f32[2,32,128]{2,1,0:T(8,128)S(1)} %pad_maximum_fusion.8), channel_id=1, source_target_pairs={{0,28},{2,30},{4,0},{6,2},{8,4},{10,6},{12,8},{14,10},{16,12},{18,... | collective-permute-start | bytes 98312 | tf_op jit(solution)/shard_map/ppermute | solution.py:12
  116.4 4.8 %collective-permute-start.10 = (f32[4,32,128]{2,1,0:T(8,128)S(1)}, f32[4,32,128]{2,1,0:T(8,128)S(1)}, u32[]{:S(2)}, u32[]{:S(2)}) collective-permute-start(f32[4,32,128]{2,1,0:T(8,128)S(1)} %pad_maximum_fusion.7), channel_id=1, source_target_pairs={{0,24},{2,26},{4,28},{6,30},{8,0},{10,2},{12,4},{14,6},{16,8},{18,... | collective-permute-start | bytes 196616 | tf_op jit(solution)/shard_map/ppermute | solution.py:12
  121.9 8.1 %all-to-all-start.2 = ((f32[5,32,2,128]{3,1,0,2:T(8,128)}), f32[5,32,2,128]{3,1,0,2:T(8,128)S(1)}, u32[]{:S(2)}, u32[]{:S(2)}) async-start(f32[5,32,2,128]{3,1,0,2:T(8,128)} %copy.37), calls=%async_computation.2 | async-start | bytes 327680 | tf_op jit(solution)/shard_map/all_to_all | solution.py:63
  125.3 6.6 %collective-permute-start.7 = (f32[32,128]{1,0:T(8,128)S(1)}, f32[32,128]{1,0:T(8,128)S(1)}, u32[]{:S(2)}, u32[]{:S(2)}) collective-permute-start(f32[32,128]{1,0:T(8,128)S(1)} %multiply_add_fusion.1), channel_id=1, source_target_pairs={{0,16},{2,18},{4,20},{6,22},{8,24},{10,26},{12,28},{14,30},{16,0},... | collective-permute-start | bytes 49160 | tf_op jit(solution)/shard_map/ppermute | solution.py:12
  140.1 6.1 %collective-permute-start.11 = (f32[4,32,128]{2,1,0:T(8,128)S(1)}, f32[4,32,128]{2,1,0:T(8,128)S(1)}, u32[]{:S(2)}, u32[]{:S(2)}) collective-permute-start(f32[4,32,128]{2,1,0:T(8,128)S(1)} %slice.264), channel_id=1, source_target_pairs={{0,8},{2,10},{4,12},{6,14},{8,16},{10,18},{12,20},{14,22},{16,24},... | collective-permute-start | bytes 196616 | tf_op jit(solution)/shard_map/ppermute | solution.py:12
  146.2 7.0 %collective-permute-start.12 = (f32[2,32,128]{2,1,0:T(8,128)S(1)}, f32[2,32,128]{2,1,0:T(8,128)S(1)}, u32[]{:S(2)}, u32[]{:S(2)}) collective-permute-start(f32[2,32,128]{2,1,0:T(8,128)S(1)} %slice.266), channel_id=1, source_target_pairs={{0,4},{2,6},{4,8},{6,10},{8,12},{10,14},{12,16},{14,18},{16,20},{1... | collective-permute-start | bytes 98312 | tf_op jit(solution)/shard_map/ppermute | solution.py:12
  153.2 5.9 %collective-permute-start.13 = (f32[1,32,128]{2,1,0:T(8,128)S(1)}, f32[1,32,128]{2,1,0:T(8,128)S(1)}, u32[]{:S(2)}, u32[]{:S(2)}) collective-permute-start(f32[1,32,128]{2,1,0:T(8,128)S(1)} %slice.268), channel_id=1, source_target_pairs={{0,2},{2,4},{4,6},{6,8},{8,10},{10,12},{12,14},{14,16},{16,18},{18... | collective-permute-start | bytes 49160 | tf_op jit(solution)/shard_map/ppermute | solution.py:12
where the time goes:
time: 198 us; the launch traced here: 197 us
  blocking collectives  87.8 us (44%)
  waiting for transfers between devices  65.8 us (33%)
  starting transfers between devices  28.9 us (15%)
  matrix products  7.27 us (4%)
  between operations  2.56 us (1%)
  other arithmetic  2.3 us (1%)
  local copies, waits for them, and re-layouts  2.17 us (1%)
    psum x2, blocking collectives, on_device(): lax.psum((jnp.sum(direction * image, axis=1), jnp.sum(residual * image, a...  73.8 us
    ppermute x14, waiting for transfers between devices, from_behind(): return lax.ppermute(value, axis, pairs)  58.1 us
    ppermute x14, starting transfers between devices, from_behind(): return lax.ppermute(value, axis, pairs)  21.9 us
    all_to_all x2, blocking collectives, on_device(): lax.all_to_all(pieces, 'row', split_axis=2, concat_axis=2, tiled=True)  14 us
    all_to_all x2, waiting for transfers between devices, assemble(): lax.all_to_all(outgoing, 'row', split_axis=2, concat_axis=2, tiled=True)  7.74 us
    all_to_all x2, starting transfers between devices, assemble(): lax.all_to_all(outgoing, 'row', split_axis=2, concat_axis=2, tiled=True)  6.96 us
  transfers between devices with their start and end apart: 16, of which 15 were waited for; matrix products, arithmetic and copies ran while one was open for 1% of the time, Pallas kernels for 0%

commit v1 on v0

--- a/solution.py
+++ b/solution.py
@@ -1,6 +1,10 @@
+import functools
+
 import jax
 import jax.numpy as jnp
 from jax import lax
+from jax.experimental import pallas as pl
+from jax.experimental.pallas import tpu as pltpu
 from jax.sharding import PartitionSpec as P
 
 ITERS = 2
@@ -137,11 +141,313 @@
     return (solution, residual)
 
 
+MESH = pl.DeviceIdType.MESH
+VMEM_BUDGET = 48 * 2**20
+CORES = 2
+SIDE = 2
+
+
+def flip(index, mask):
+    bit = 1
+    while bit <= mask:
+        if mask & bit:
+            index = index + bit - 2 * bit * lax.rem(lax.div(index, bit), 2)
+        bit *= 2
+    return index
+
+
+def halves(value):
+    high = value.astype(jnp.bfloat16)
+    low = (value - high.astype(jnp.float32)).astype(jnp.bfloat16)
+    return high, low
+
+
+def column_sums(value):
+    return jnp.sum(value, axis=1, keepdims=True)
+
+
+def fused(
+    depth,
+    points_ref, targets_ref, lengths_ref, scale_ref, noise_ref,
+    solution_ref, residual_ref,
+    stack, images, kern_high, kern_low, left, acc, direct, sums, scalars,
+    send_a, recv_a, send_b, recv_b, send_c, recv_c,
+):
+    features, local = points_ref.shape
+    rhs = targets_ref.shape[0]
+    wide, row = lax.axis_index("wide"), lax.axis_index("row")
+    core = lax.rem(wide, CORES)
+    x = lax.rem(lax.div(wide, CORES), SIDE)
+    z = lax.div(wide, CORES * SIDE)
+
+    def place(level, dx, dy, dc):
+        at_z, at_x, at_y, at_c = flip(z, level), flip(x, dx), flip(row, dy), flip(core, dc)
+        return ((at_z * SIDE + at_x) * CORES + at_c, at_y)
+
+    def slot(level, dx, dy, dc):
+        at_wide, at_row = place(level, dx, dy, dc)
+        return at_wide * SIDE + at_row
+
+    plane = [(dx, dy) for dx in range(SIDE) for dy in range(SIDE)]
+    beside = [(dx, dy, dc) for dx, dy in plane for dc in range(CORES) if dx + dy + dc > 0]
+
+    barrier = pltpu.get_barrier_semaphore()
+    peers = [place(level, 0, 0, 0) for level in range(1, depth)] + [place(0, *p) for p in beside]
+    for peer in peers:
+        pl.semaphore_signal(barrier, inc=1, device_id=peer, device_id_type=MESH)
+
+    lengths = jnp.broadcast_to(lengths_ref[...], (features, features)).T
+    own = points_ref[...] / lengths[:, :local]
+    mine = slot(0, 0, 0, 0)
+    stack[mine, :features, :] = own
+    stack[mine, features:, :] = targets_ref[...]
+    pl.semaphore_wait(barrier, len(peers))
+
+    def gather(buffer, sends, recvs, use):
+        started = []
+
+        def copy(from_slot, to, number):
+            made = pltpu.make_async_remote_copy(
+                src_ref=buffer.at[from_slot],
+                dst_ref=buffer.at[from_slot],
+                send_sem=sends.at[number],
+                recv_sem=recvs.at[from_slot],
+                device_id=to,
+                device_id_type=MESH,
+            )
+            made.start()
+            started.append(made)
+
+        def arrived(at):
+            pltpu.make_async_remote_copy(
+                src_ref=buffer.at[at],
+                dst_ref=buffer.at[at],
+                send_sem=sends.at[0],
+                recv_sem=recvs.at[at],
+                device_id=place(0, 0, 0, 1),
+                device_id_type=MESH,
+            ).wait_recv()
+
+        side_x, side_y, sibling = place(0, 1, 0, 0), place(0, 0, 1, 0), place(0, 0, 0, 1)
+        for level in range(depth):
+            base = level * 8
+            here = slot(level, 0, 0, 0)
+            if level > 0:
+                arrived(here)
+            copy(here, side_x, base)
+            copy(here, side_y, base + 1)
+            if level == 0:
+                for other in range(1, depth):
+                    copy(here, place(other, 0, 0, 0), depth * 8 + other)
+            copy(here, sibling, base + 2)
+            if level > 0:
+                finish(level - 1, buffer, arrived, copy, use)
+        finish(depth - 1, buffer, arrived, copy, use)
+        return started
+
+    def finish(level, buffer, arrived, copy, use):
+        base = level * 8
+        side_x, side_y, sibling = place(0, 1, 0, 0), place(0, 0, 1, 0), place(0, 0, 0, 1)
+        from_x, from_y, from_d = slot(level, 1, 0, 0), slot(level, 0, 1, 0), slot(level, 1, 1, 0)
+        arrived(from_x)
+        if level % 2 == 0:
+            copy(from_x, side_y, base + 3)
+        copy(from_x, sibling, base + 4)
+        arrived(from_y)
+        if level % 2 == 1:
+            copy(from_y, side_x, base + 3)
+        copy(from_y, sibling, base + 5)
+        arrived(from_d)
+        copy(from_d, sibling, base + 6)
+        use(level, 0)
+        for dx, dy in plane:
+            arrived(slot(level, dx, dy, 1))
+        use(level, 1)
+
+    own_t = own.T
+    high, low = halves(own_t)
+    left[:local, :features] = high
+    left[:local, features:] = high
+    left[local:, :features] = low
+    left[local:, features:] = low
+    own_sq = column_sums(own_t * own_t)
+    kern_scale = scale_ref[0]
+    noise_var = noise_ref[0]
+    acc[...] = jnp.zeros_like(acc)
+
+    def group(level, dc):
+        return [slot(level, dx, dy, dc) for dx, dy in plane]
+
+    def apply(vectors, first):
+        total = None
+        for at, vector in enumerate(vectors):
+            vec_high, vec_low = halves(vector)
+            tile_high, tile_low = kern_high[first + at], kern_low[first + at]
+            part = lax.dot_general(
+                jnp.concatenate([vec_high, vec_low], axis=1),
+                jnp.concatenate([tile_high, tile_high], axis=1),
+                (((1,), (1,)), ((), ())),
+                preferred_element_type=jnp.float32,
+            ) + lax.dot_general(
+                vec_high, tile_low, (((1,), (1,)), ((), ())), preferred_element_type=jnp.float32
+            )
+            total = part if total is None else total + part
+        return total
+
+    def build(level, dc):
+        first = (level * CORES + dc) * len(plane)
+        slots = group(level, dc)
+        for at, place_at in enumerate(slots):
+            block = stack[place_at, :features, :]
+            block_high, block_low = halves(block)
+            product = jnp.dot(
+                left[...],
+                jnp.concatenate([block_high, block_low], axis=0),
+                preferred_element_type=jnp.float32,
+            )
+            cross = product[:local] + product[local:]
+            block_sq = jnp.sum(block * block, axis=0, keepdims=True)
+            tile = kern_scale * jnp.exp(-0.5 * (own_sq + block_sq - 2.0 * cross))
+            tile_high, tile_low = halves(tile)
+            kern_high[first + at] = tile_high
+            kern_low[first + at] = tile_low
+        vectors = [stack[place_at, features:, :] for place_at in slots]
+        acc[...] += apply(vectors, first)
+        sums[0] += sum(vector * vector for vector in vectors)
+
+    sums[...] = jnp.zeros_like(sums)
+    copies = gather(stack, send_a, recv_a, build)
+    targets = targets_ref[...]
+    images[mine] = acc[...] + noise_var * targets
+
+    def curve(level, dc):
+        sums[1] += sum(
+            stack[place_at, features:, :] * images[place_at] for place_at in group(level, dc)
+        )
+
+    copies += gather(images, send_b, recv_b, curve)
+    norm_now = column_sums(sums[0])
+    step_size = norm_now / column_sums(sums[1])
+    wide_step = jnp.broadcast_to(step_size, (rhs, local))
+    count = depth * CORES * len(plane)
+    total = jnp.zeros((rhs, local), jnp.float32)
+    order = [s for level in range(depth) for dc in range(CORES) for s in group(level, dc)]
+    for at, place_at in enumerate(order):
+        left_over = stack[place_at, features:, :] - wide_step * images[place_at]
+        direct[at] = left_over
+        total += left_over * left_over
+    norm_next = column_sums(total)
+    ratio = jnp.broadcast_to(norm_next / norm_now, (rhs, local))
+    image = jnp.zeros((rhs, local), jnp.float32)
+    for first in range(0, count, len(plane)):
+        vectors = [
+            direct[first + at] + ratio * stack[order[first + at], features:, :]
+            for at in range(len(plane))
+        ]
+        image += apply(vectors, first)
+    residual = targets - wide_step * images[mine]
+    direction = residual + ratio * targets
+    image += noise_var * direction
+
+    padded = jnp.concatenate(
+        [direction * image, jnp.zeros((local - rhs, local), jnp.float32)], axis=0
+    )
+    curves = jnp.broadcast_to(jnp.sum(padded.T, axis=0, keepdims=True), (8, local))
+
+    def exchange(value, base, partners):
+        curve_ref = scalars.at[base]
+        curve_ref[...] = value
+        made = []
+        for at, partner in enumerate(partners):
+            made.append(
+                pltpu.make_async_remote_copy(
+                    src_ref=curve_ref,
+                    dst_ref=scalars.at[base + 1 + at],
+                    send_sem=send_c.at[base + at],
+                    recv_sem=recv_c.at[base + at],
+                    device_id=partner,
+                    device_id_type=MESH,
+                )
+            )
+            made[-1].start()
+        for at, one in enumerate(made):
+            one.wait_recv()
+            value = value + scalars.at[base + 1 + at][...]
+        copies.extend(made)
+        return value
+
+    curves = exchange(curves, 0, [place(level, 0, 0, 0) for level in range(1, depth)])
+    curves = exchange(curves, depth, [place(0, *p) for p in beside])
+    spread = jnp.broadcast_to(curves[:1], (local, local)).T[:rhs]
+    last_step = jnp.broadcast_to(norm_next, (rhs, local)) / spread
+    solution_ref[...] = wide_step * targets + last_step * direction
+    residual_ref[...] = residual - last_step * image
+    for one in copies:
+        one.wait_send()
+
+
+def on_device_fused(points, targets, lengthscales, outputscale, noise):
+    features, local = points.shape
+    rhs = targets.shape[0]
+    devices = lax.axis_size("wide") * lax.axis_size("row")
+    depth = lax.axis_size("wide") // (CORES * SIDE)
+    vmem, smem = pl.BlockSpec(memory_space=pltpu.VMEM), pl.BlockSpec(memory_space=pltpu.SMEM)
+    own = jax.ShapeDtypeStruct((rhs, local), jnp.float32)
+    peers = depth - 1 + 2 * SIDE * SIDE - 1
+    dma = pltpu.SemaphoreType.DMA
+    return pl.pallas_call(
+        functools.partial(fused, depth),
+        out_shape=(own, own),
+        in_specs=[vmem, vmem, vmem, smem, smem],
+        out_specs=(vmem, vmem),
+        scratch_shapes=[
+            pltpu.VMEM((devices, features + rhs, local), jnp.float32),
+            pltpu.VMEM((devices, rhs, local), jnp.float32),
+            pltpu.VMEM((devices, local, local), jnp.bfloat16),
+            pltpu.VMEM((devices, local, local), jnp.bfloat16),
+            pltpu.VMEM((2 * local, 2 * features), jnp.bfloat16),
+            pltpu.VMEM((rhs, local), jnp.float32),
+            pltpu.VMEM((devices, rhs, local), jnp.float32),
+            pltpu.VMEM((2, rhs, local), jnp.float32),
+            pltpu.VMEM((peers + 2, 8, local), jnp.float32),
+            dma((9 * depth,)),
+            dma((devices,)),
+            dma((9 * depth,)),
+            dma((devices,)),
+            dma((peers + 2,)),
+            dma((peers + 2,)),
+        ],
+        compiler_params=pltpu.CompilerParams(
+            collective_id=0, has_side_effects=True, vmem_limit_bytes=VMEM_BUDGET
+        ),
+    )(points, targets, lengthscales[None, :], outputscale, noise)
+
+
 def solution(mesh):
-    return jax.shard_map(
-        on_device,
-        mesh=mesh,
-        in_specs=(P(None, ("wide", "row")), P(None, ("wide", "row")), P(), P(), P()),
-        out_specs=(P(None, ("wide", "row")), P(None, ("wide", "row"))),
-        check_vma=False,
-    )
+    sizes = dict(mesh.shape)
+    devices = sizes["wide"] * sizes["row"]
+    depth = sizes["wide"] // (CORES * SIDE)
+
+    def whole(points, targets, lengthscales, outputscale, noise):
+        features, count = points.shape
+        rhs = targets.shape[0]
+        local = count // devices
+        held = 4 * count * (features + 3 * rhs + local)
+        fits = (
+            sizes["row"] == SIDE
+            and sizes["wide"] == depth * CORES * SIDE
+            and depth & (depth - 1) == 0
+            and local == features
+            and rhs <= local
+            and 2 * held <= VMEM_BUDGET
+        )
+        own = P(None, ("wide", "row"))
+        return jax.shard_map(
+            on_device_fused if fits else on_device,
+            mesh=mesh,
+            in_specs=(own, own, P(), P(), P()),
+            out_specs=(own, own),
+            check_vma=False,
+        )(points, targets, lengthscales, outputscale, noise)
+
+    return whole

time: 198 us -> 68.4 us (0.35)
  blocking collectives: 87.8 us -> 0 us
  waiting for transfers between devices: 65.8 us -> 0 us
  Pallas kernels: 0 us -> 62.8 us
  starting transfers between devices: 28.9 us -> 0 us
  matrix products: 7.27 us -> 0 us
  other arithmetic: 2.3 us -> 0 us
    psum x2 -> x0, blocking collectives: 73.8 us -> none  [on_device(): lax.psum((jnp.sum(direction * image, axis=1), jnp.sum(residual * image, a...]
    pallas_call x0 -> x1, Pallas kernels: none -> 62.8 us  [on_device_fused(): pl.pallas_call(functools.partial(fused, depth), out_shape=(own, own), in_...]
    ppermute x14 -> x0, waiting for transfers between devices: 58.1 us -> none  [from_behind(): return lax.ppermute(value, axis, pairs)]
    ppermute x14 -> x0, starting transfers between devices: 21.9 us -> none  [from_behind(): return lax.ppermute(value, axis, pairs)]
    all_to_all x2 -> x0, blocking collectives: 14 us -> none  [on_device(): lax.all_to_all(pieces, 'row', split_axis=2, concat_axis=2, tiled=True)]
    all_to_all x2 -> x0, waiting for transfers between devices: 7.74 us -> none  [assemble(): lax.all_to_all(outgoing, 'row', split_axis=2, concat_axis=2, tiled=True)]
    dot_general x23 -> x0, matrix products: 7.27 us -> none  [the longest x10 3.22 us: apply_rows(): lax.dot_general(vectors, kernel, (((1,), (1,)), ((), ())), precision=lax....]
    all_to_all x2 -> x0, starting transfers between devices: 6.96 us -> none  [assemble(): lax.all_to_all(outgoing, 'row', split_axis=2, concat_axis=2, tiled=True)]
  transfers between devices with their start and end apart: 16 -> 0, of which waited for: 15 -> 0; matrix products, arithmetic and copies ran while one was open for 1% -> 0% of each run, Pallas kernels for 0% -> 0%
where the time goes in v1:
time: 68.4 us; the launch traced here: 68.2 us
  Pallas kernels  62.8 us (92%)
  local copies, waits for them, and re-layouts  3.42 us (5%)
  between operations  1.94 us (3%)
    pallas_call x1, Pallas kernels, on_device_fused(): pl.pallas_call(functools.partial(fused, depth), out_shape=(own, own), in_...  62.8 us
    unnamed x8, local copies, waits for them, and re-layouts  3.42 us

profile of v1, /device:TPU:0, one launch (start us, length us, event | category | flops | bytes accessed | tf_op | source)
XLA Modules:
  0.0 68.2 jit_solution(15441798000329284707)
XLA Ops:
  1.9 0.0 copy-start.2
  1.9 0.6 copy-done.2
  2.6 0.0 copy-start
  2.6 0.8 %copy-done = f32[128,128]{1,0:T(8,128)S(1)} copy-done((f32[128,128]{1,0:T(8,128)S(1)}, f32[128,128]{1,0:T(8,128)}, u32[]{:S(2)}) %copy-start) | copy-done | bytes 65560
  3.4 0.0 copy-start.1
  3.4 0.7 %copy-done.1 = f32[32,128]{1,0:T(8,128)S(1)} copy-done((f32[32,128]{1,0:T(8,128)S(1)}, f32[32,128]{1,0:T(8,128)}, u32[]{:S(2)}) %copy-start.1) | copy-done | bytes 16408
  4.1 62.8 %shard_map.68 = (f32[32,128]{1,0:T(8,128)S(1)}, f32[32,128]{1,0:T(8,128)S(1)}) custom-call(f32[128,128]{1,0:T(8,128)S(1)} %copy-done, f32[32,128]{1,0:T(8,128)S(1)} %copy-done.1, f32[1,128]{1,0:T(1,128)S(1)} %bitcast.1, f32[1]{0:T(128)S(6)} %copy.9.scale_ref, f32[1]{0:T(128)S(6)} %copy.10.noise_ref), custom_call_target="tpu_custom_call" | custom-call | tf_op jit(solution)/shard_map/pallas_call | solution.py:398
  67.0 0.6 copy.11
  67.6 0.6 copy.12
Async XLA Ops:
  1.9 0.7 copy-start.2
  2.6 0.8 %copy-start = (f32[128,128]{1,0:T(8,128)S(1)}, f32[128,128]{1,0:T(8,128)}, u32[]{:S(2)}) copy-start(f32[128,128]{1,0:T(8,128)} %points_ref.1) | copy-start | bytes 196612
  3.4 0.7 %copy-start.1 = (f32[32,128]{1,0:T(8,128)S(1)}, f32[32,128]{1,0:T(8,128)}, u32[]{:S(2)}) copy-start(f32[32,128]{1,0:T(8,128)} %targets_ref.1) | copy-start | bytes 49156

commit v2 on v1

--- a/solution.py
+++ b/solution.py
@@ -228,41 +228,28 @@
                 device_id_type=MESH,
             ).wait_recv()
 
-        side_x, side_y, sibling = place(0, 1, 0, 0), place(0, 0, 1, 0), place(0, 0, 0, 1)
+        sibling = place(0, 0, 0, 1)
+        across = [(dx, dy) for dx, dy in plane if dx + dy > 0]
         for level in range(depth):
-            base = level * 8
             here = slot(level, 0, 0, 0)
             if level > 0:
                 arrived(here)
-            copy(here, side_x, base)
-            copy(here, side_y, base + 1)
-            if level == 0:
+            else:
                 for other in range(1, depth):
                     copy(here, place(other, 0, 0, 0), depth * 8 + other)
-            copy(here, sibling, base + 2)
-            if level > 0:
-                finish(level - 1, buffer, arrived, copy, use)
-        finish(depth - 1, buffer, arrived, copy, use)
+            for at, (dx, dy) in enumerate(across):
+                copy(here, place(0, dx, dy, 0), level * 8 + at)
+            copy(here, sibling, level * 8 + 3)
+        for level in range(depth):
+            for at, (dx, dy) in enumerate(across):
+                landed = slot(level, dx, dy, 0)
+                arrived(landed)
+                copy(landed, sibling, level * 8 + 4 + at)
+            use(level, 0)
+            for dx, dy in plane:
+                arrived(slot(level, dx, dy, 1))
+            use(level, 1)
         return started
-
-    def finish(level, buffer, arrived, copy, use):
-        base = level * 8
-        side_x, side_y, sibling = place(0, 1, 0, 0), place(0, 0, 1, 0), place(0, 0, 0, 1)
-        from_x, from_y, from_d = slot(level, 1, 0, 0), slot(level, 0, 1, 0), slot(level, 1, 1, 0)
-        arrived(from_x)
-        if level % 2 == 0:
-            copy(from_x, side_y, base + 3)
-        copy(from_x, sibling, base + 4)
-        arrived(from_y)
-        if level % 2 == 1:
-            copy(from_y, side_x, base + 3)
-        copy(from_y, sibling, base + 5)
-        arrived(from_d)
-        copy(from_d, sibling, base + 6)
-        use(level, 0)
-        for dx, dy in plane:
-            arrived(slot(level, dx, dy, 1))
-        use(level, 1)
 
     own_t = own.T
     high, low = halves(own_t)

time: 68.4 us -> 48.1 us (0.70)
  Pallas kernels: 62.8 us -> 42.5 us
    pallas_call x1, Pallas kernels: 62.8 us -> 42.5 us  [on_device_fused(): pl.pallas_call(functools.partial(fused, depth), out_shape=(own, own), in_...]
where the time goes in v2:
time: 48.1 us; the launch traced here: 47.8 us
  Pallas kernels  42.5 us (88%)
  local copies, waits for them, and re-layouts  3.42 us (7%)
  between operations  1.94 us (4%)
    pallas_call x1, Pallas kernels, on_device_fused(): pl.pallas_call(functools.partial(fused, depth), out_shape=(own, own), in_...  42.5 us
    unnamed x8, local copies, waits for them, and re-layouts  3.42 us

profile of v2, /device:TPU:0, one launch (start us, length us, event | category | flops | bytes accessed | tf_op | source)
XLA Modules:
  0.0 47.8 jit_solution(6474253518216375561)
XLA Ops:
  1.9 0.0 copy-start.2
  1.9 0.6 %copy-done.2 = f32[128]{0:T(128)S(1)} copy-done((f32[128]{0:T(128)S(1)}, f32[128]{0:T(128)}, u32[]{:S(2)}) %copy-start.2) | copy-done | bytes 536
  2.6 0.0 copy-start
  2.6 0.8 %copy-done = f32[128,128]{1,0:T(8,128)S(1)} copy-done((f32[128,128]{1,0:T(8,128)S(1)}, f32[128,128]{1,0:T(8,128)}, u32[]{:S(2)}) %copy-start) | copy-done | bytes 65560
  3.4 0.0 copy-start.1
  3.4 0.7 %copy-done.1 = f32[32,128]{1,0:T(8,128)S(1)} copy-done((f32[32,128]{1,0:T(8,128)S(1)}, f32[32,128]{1,0:T(8,128)}, u32[]{:S(2)}) %copy-start.1) | copy-done | bytes 16408
  4.1 42.5 %shard_map.68 = (f32[32,128]{1,0:T(8,128)S(1)}, f32[32,128]{1,0:T(8,128)S(1)}) custom-call(f32[128,128]{1,0:T(8,128)S(1)} %copy-done, f32[32,128]{1,0:T(8,128)S(1)} %copy-done.1, f32[1,128]{1,0:T(1,128)S(1)} %bitcast.1, f32[1]{0:T(128)S(6)} %copy.9.scale_ref, f32[1]{0:T(128)S(6)} %copy.10.noise_ref), custom_call_target="tpu_custom_call" | custom-call | tf_op jit(solution)/shard_map/pallas_call | solution.py:385
  46.6 0.6 %copy.11 = f32[32,128]{1,0:T(8,128)} copy(f32[32,128]{1,0:T(8,128)S(1)} %get-tuple-element.4) | data formatting | bytes 32768
  47.2 0.6 %copy.12 = f32[32,128]{1,0:T(8,128)} copy(f32[32,128]{1,0:T(8,128)S(1)} %get-tuple-element.5) | data formatting | bytes 32768
Async XLA Ops:
  1.9 0.7 %copy-start.2 = (f32[128]{0:T(128)S(1)}, f32[128]{0:T(128)}, u32[]{:S(2)}) copy-start(f32[128]{0:T(128)} %param.7) | copy-start | bytes 1540
  2.6 0.8 %copy-start = (f32[128,128]{1,0:T(8,128)S(1)}, f32[128,128]{1,0:T(8,128)}, u32[]{:S(2)}) copy-start(f32[128,128]{1,0:T(8,128)} %points_ref.1) | copy-start | bytes 196612
  3.4 0.7 %copy-start.1 = (f32[32,128]{1,0:T(8,128)S(1)}, f32[32,128]{1,0:T(8,128)}, u32[]{:S(2)}) copy-start(f32[32,128]{1,0:T(8,128)} %targets_ref.1) | copy-start | bytes 49156

commit v3 on v0

--- a/solution.py
+++ b/solution.py
@@ -1,6 +1,10 @@
+import functools
+
 import jax
 import jax.numpy as jnp
 from jax import lax
+from jax.experimental import pallas as pl
+from jax.experimental.pallas import tpu as pltpu
 from jax.sharding import PartitionSpec as P
 
 ITERS = 2
@@ -137,11 +141,286 @@
     return (solution, residual)
 
 
+MESH = pl.DeviceIdType.MESH
+VMEM_BUDGET = 48 * 2**20
+CORES = 2
+SIDE = 2
+
+
+def flip(index, mask):
+    bit = 1
+    while bit <= mask:
+        if mask & bit:
+            index = index + bit - 2 * bit * lax.rem(lax.div(index, bit), 2)
+        bit *= 2
+    return index
+
+
+def halves(value):
+    high = value.astype(jnp.bfloat16)
+    low = (value - high.astype(jnp.float32)).astype(jnp.bfloat16)
+    return high, low
+
+
+def column_sums(value):
+    return jnp.sum(value, axis=1, keepdims=True)
+
+
+def fused(
+    depth,
+    points_ref, targets_ref, lengths_ref, scale_ref, noise_ref,
+    solution_ref, residual_ref,
+    stack, images, kern_high, kern_low, parts, landing, scalars,
+    send_a, recv_a, send_b, recv_b, send_p, recv_p, send_s, recv_s,
+):
+    features, local = points_ref.shape
+    rhs = targets_ref.shape[0]
+    wide, row = lax.axis_index("wide"), lax.axis_index("row")
+    core = lax.rem(wide, CORES)
+    x = lax.rem(lax.div(wide, CORES), SIDE)
+    z = lax.div(wide, CORES * SIDE)
+    plane = [(dx, dy, dc) for dc in range(CORES) for dx in range(SIDE) for dy in range(SIDE)]
+    across = [(dx, dy, 0) for dx in range(SIDE) for dy in range(SIDE) if dx + dy > 0]
+    width = len(plane)
+    everyone = [(level, *at) for level in range(depth) for at in plane][1:]
+
+    def place(level, dx, dy, dc):
+        at_z, at_x, at_y, at_c = flip(z, level), flip(x, dx), flip(row, dy), flip(core, dc)
+        return ((at_z * SIDE + at_x) * CORES + at_c, at_y)
+
+    def number(dx, dy, dc):
+        return plane.index((dx, dy, dc))
+
+    barrier = pltpu.get_barrier_semaphore()
+    for peer in everyone:
+        pl.semaphore_signal(barrier, inc=1, device_id=place(*peer), device_id_type=MESH)
+
+    lengths = jnp.broadcast_to(lengths_ref[...], (features, features)).T
+    targets = targets_ref[...]
+    stack[0, :features, :] = points_ref[...] / lengths[:, :local]
+    stack[0, features:, :] = targets
+    images[0] = jnp.zeros_like(targets)
+    pl.semaphore_wait(barrier, len(everyone))
+
+    started = []
+
+    def copy(source, target, sends, sent, recvs, received, to):
+        made = pltpu.make_async_remote_copy(
+            src_ref=source,
+            dst_ref=target,
+            send_sem=sends.at[sent],
+            recv_sem=recvs.at[received],
+            device_id=place(*to),
+            device_id_type=MESH,
+        )
+        made.start()
+        started.append(made)
+        return made
+
+    def spread(buffer, sends, recvs):
+        column, beside = {}, {}
+        for level in range(1, depth):
+            at = width + level - 1
+            column[level] = copy(buffer.at[0], buffer.at[at], sends, at, recvs, at, (level, 0, 0, 0))
+        for to in across:
+            at = number(*to)
+            beside[to] = copy(buffer.at[0], buffer.at[at], sends, at, recvs, at, (0, *to))
+        at = number(0, 0, 1)
+        beside[0, 0, 1] = copy(buffer.at[0], buffer.at[at], sends, at, recvs, at, (0, 0, 0, 1))
+        return column, beside
+
+    def relay(buffer, sends, recvs, beside):
+        for to in across:
+            beside[to].wait_recv()
+            at = number(to[0], to[1], 1)
+            beside[to[0], to[1], 1] = copy(
+                buffer.at[number(*to)], buffer.at[at], sends, at, recvs, at, (0, 0, 0, 1)
+            )
+        for at in plane[SIDE * SIDE :]:
+            beside[at].wait_recv()
+
+    kern_scale = scale_ref[0]
+    noise_var = noise_ref[0]
+
+    def apply(vectors, level):
+        total = None
+        for at, (vec_high, vec_low) in enumerate(vectors):
+            tile_high, tile_low = kern_high[level * width + at], kern_low[level * width + at]
+            part = lax.dot_general(
+                jnp.concatenate([vec_high, vec_low], axis=1),
+                jnp.concatenate([tile_high, tile_high], axis=1),
+                (((1,), (1,)), ((), ())),
+                preferred_element_type=jnp.float32,
+            ) + lax.dot_general(
+                vec_high, tile_low, (((1,), (1,)), ((), ())), preferred_element_type=jnp.float32
+            )
+            total = part if total is None else total + part
+        return total
+
+    def build(level):
+        own = stack[0 if level == 0 else width + level - 1, :features, :].T
+        own_sq = column_sums(own * own)
+        high, low = halves(own)
+        left = jnp.concatenate(
+            [jnp.concatenate([high, high], axis=1), jnp.concatenate([low, low], axis=1)], axis=0
+        )
+        for at in range(width):
+            block = stack[at, :features, :]
+            block_high, block_low = halves(block)
+            product = jnp.dot(
+                left,
+                jnp.concatenate([block_high, block_low], axis=0),
+                preferred_element_type=jnp.float32,
+            )
+            cross = product[:local] + product[local:]
+            block_sq = jnp.sum(block * block, axis=0, keepdims=True)
+            tile = kern_scale * jnp.exp(-0.5 * (own_sq + block_sq - 2.0 * cross))
+            tile_high, tile_low = halves(tile)
+            kern_high[level * width + at] = tile_high
+            kern_low[level * width + at] = tile_low
+
+    def send_part(turn, level, value):
+        at = turn * depth + level
+        parts[at] = value
+        return copy(parts.at[at], landing.at[at], send_p, at, recv_p, at, (level, 0, 0, 0))
+
+    def send_scalars(turn, values):
+        pad = jnp.zeros((local - len(values) * rhs, local), jnp.float32)
+        sums = jnp.sum(jnp.concatenate([*values, pad], axis=0).T, axis=0, keepdims=True)
+        base = turn * (len(everyone) + 1)
+        scalars[base] = jnp.broadcast_to(sums, scalars.shape[1:])
+        return [
+            copy(scalars.at[base], scalars.at[base + 1 + at], send_s, base + 1 + at, recv_s, base + 1 + at, peer)
+            for at, peer in enumerate(everyone)
+        ]
+
+    def all_scalars(turn, copies):
+        for one in copies:
+            one.wait_recv()
+        base = turn * (len(everyone) + 1)
+        total = scalars[base]
+        for at in range(len(everyone)):
+            total = total + scalars[base + 1 + at]
+        return jnp.broadcast_to(total[:1], (local, local)).T
+
+    column, beside = spread(stack, send_a, recv_a)
+    relay(stack, send_a, recv_a, beside)
+    vectors = [halves(stack[at, features:, :]) for at in range(width)]
+    build(0)
+    mine = apply(vectors, 0)
+    sent = []
+    for level in range(1, depth):
+        column[level].wait_recv()
+        build(level)
+        sent.append(send_part(0, level, apply(vectors, level)))
+    for one in sent:
+        one.wait_recv()
+    for level in range(1, depth):
+        mine = mine + landing[level]
+    first_image = mine + noise_var * targets
+    images[0] = first_image
+    column, beside = spread(images, send_b, recv_b)
+    sent = send_scalars(0, [targets * targets, targets * first_image, first_image * first_image])
+    relay(images, send_b, recv_b, beside)
+    for level in range(1, depth):
+        column[level].wait_recv()
+    found = all_scalars(0, sent)
+    norm_now, curve, image_sq = found[:rhs], found[rhs : 2 * rhs], found[2 * rhs : 3 * rhs]
+    step = norm_now / curve
+    norm_next = norm_now - 2.0 * step * curve + step * step * image_sq
+    ratio = norm_next / norm_now
+
+    def turned(at):
+        vector = stack[at, features:, :]
+        return (vector - step * images[at]) + ratio * vector
+
+    vectors = [halves(turned(at)) for at in range(width)]
+    direction = turned(0)
+    sent = []
+    weighted = noise_var * direction * direction
+    for level in range(1, depth):
+        part = apply(vectors, level)
+        sent.append(send_part(1, level, part))
+        weighted += turned(width + level - 1) * part
+    mine = apply(vectors, 0)
+    weighted += direction * mine
+    sums = send_scalars(1, [weighted])
+    for one in sent:
+        one.wait_recv()
+    for level in range(1, depth):
+        mine = mine + landing[depth + level]
+    image = mine + noise_var * direction
+    residual = targets - step * first_image
+    last_step = norm_next / all_scalars(1, sums)[:rhs]
+    solution_ref[...] = step * targets + last_step * direction
+    residual_ref[...] = residual - last_step * image
+    for one in started:
+        one.wait_send()
+
+
+def on_device_fused(points, targets, lengthscales, outputscale, noise):
+    features, local = points.shape
+    rhs = targets.shape[0]
+    devices = lax.axis_size("wide") * lax.axis_size("row")
+    depth = lax.axis_size("wide") // (CORES * SIDE)
+    vmem, smem = pl.BlockSpec(memory_space=pltpu.VMEM), pl.BlockSpec(memory_space=pltpu.SMEM)
+    own = jax.ShapeDtypeStruct((rhs, local), jnp.float32)
+    width = SIDE * SIDE * CORES
+    near = width + depth - 1
+    dma = pltpu.SemaphoreType.DMA
+    return pl.pallas_call(
+        functools.partial(fused, depth),
+        out_shape=(own, own),
+        in_specs=[vmem, vmem, vmem, smem, smem],
+        out_specs=(vmem, vmem),
+        scratch_shapes=[
+            pltpu.VMEM((near, features + rhs, local), jnp.float32),
+            pltpu.VMEM((near, rhs, local), jnp.float32),
+            pltpu.VMEM((depth * width, local, local), jnp.bfloat16),
+            pltpu.VMEM((depth * width, local, local), jnp.bfloat16),
+            pltpu.VMEM((2 * depth, rhs, local), jnp.float32),
+            pltpu.VMEM((2 * depth, rhs, local), jnp.float32),
+            pltpu.VMEM((2 * devices, 8, local), jnp.float32),
+            dma((near,)),
+            dma((near,)),
+            dma((near,)),
+            dma((near,)),
+            dma((2 * depth,)),
+            dma((2 * depth,)),
+            dma((2 * devices,)),
+            dma((2 * devices,)),
+        ],
+        compiler_params=pltpu.CompilerParams(
+            collective_id=0, has_side_effects=True, vmem_limit_bytes=VMEM_BUDGET
+        ),
+    )(points, targets, lengthscales[None, :], outputscale, noise)
+
+
 def solution(mesh):
-    return jax.shard_map(
-        on_device,
-        mesh=mesh,
-        in_specs=(P(None, ("wide", "row")), P(None, ("wide", "row")), P(), P(), P()),
-        out_specs=(P(None, ("wide", "row")), P(None, ("wide", "row"))),
-        check_vma=False,
-    )
+    sizes = dict(mesh.shape)
+    devices = sizes["wide"] * sizes["row"]
+    depth = sizes["wide"] // (CORES * SIDE)
+
+    def whole(points, targets, lengthscales, outputscale, noise):
+        features, count = points.shape
+        rhs = targets.shape[0]
+        local = count // devices
+        held = 4 * count * (features + 3 * rhs + local)
+        fits = (
+            sizes["row"] == SIDE
+            and sizes["wide"] == depth * CORES * SIDE
+            and depth & (depth - 1) == 0
+            and local == features
+            and 3 * rhs <= local
+            and 2 * held <= VMEM_BUDGET
+        )
+        own = P(None, ("wide", "row"))
+        return jax.shard_map(
+            on_device_fused if fits else on_device,
+            mesh=mesh,
+            in_specs=(own, own, P(), P(), P()),
+            out_specs=(own, own),
+            check_vma=False,
+        )(points, targets, lengthscales, outputscale, noise)
+
+    return whole

time: 198 us -> 40.7 us (0.21)
  blocking collectives: 87.8 us -> 0 us
  waiting for transfers between devices: 65.8 us -> 0 us
  Pallas kernels: 0 us -> 35.1 us
  starting transfers between devices: 28.9 us -> 0 us
  matrix products: 7.27 us -> 0 us
  other arithmetic: 2.3 us -> 0 us
    psum x2 -> x0, blocking collectives: 73.8 us -> none  [on_device(): lax.psum((jnp.sum(direction * image, axis=1), jnp.sum(residual * image, a...]
    ppermute x14 -> x0, waiting for transfers between devices: 58.1 us -> none  [from_behind(): return lax.ppermute(value, axis, pairs)]
    pallas_call x0 -> x1, Pallas kernels: none -> 35.1 us  [on_device_fused(): pl.pallas_call(functools.partial(fused, depth), out_shape=(own, own), in_...]
    ppermute x14 -> x0, starting transfers between devices: 21.9 us -> none  [from_behind(): return lax.ppermute(value, axis, pairs)]
    all_to_all x2 -> x0, blocking collectives: 14 us -> none  [on_device(): lax.all_to_all(pieces, 'row', split_axis=2, concat_axis=2, tiled=True)]
    all_to_all x2 -> x0, waiting for transfers between devices: 7.74 us -> none  [assemble(): lax.all_to_all(outgoing, 'row', split_axis=2, concat_axis=2, tiled=True)]
    dot_general x23 -> x0, matrix products: 7.27 us -> none  [the longest x10 3.22 us: apply_rows(): lax.dot_general(vectors, kernel, (((1,), (1,)), ((), ())), precision=lax....]
    all_to_all x2 -> x0, starting transfers between devices: 6.96 us -> none  [assemble(): lax.all_to_all(outgoing, 'row', split_axis=2, concat_axis=2, tiled=True)]
  transfers between devices with their start and end apart: 16 -> 0, of which waited for: 15 -> 0; matrix products, arithmetic and copies ran while one was open for 1% -> 0% of each run, Pallas kernels for 0% -> 0%
where the time goes in v3:
time: 40.7 us; the launch traced here: 40.5 us
  Pallas kernels  35.1 us (86%)
  local copies, waits for them, and re-layouts  3.42 us (8%)
  between operations  1.94 us (5%)
    pallas_call x1, Pallas kernels, on_device_fused(): pl.pallas_call(functools.partial(fused, depth), out_shape=(own, own), in_...  35.1 us
    unnamed x8, local copies, waits for them, and re-layouts  3.42 us

profile of v3, /device:TPU:0, one launch (start us, length us, event | category | flops | bytes accessed | tf_op | source)
XLA Modules:
  0.0 40.5 jit_solution(16598990867185456294)
XLA Ops:
  1.9 0.0 copy-start.2
  1.9 0.6 %copy-done.2 = f32[128]{0:T(128)S(1)} copy-done((f32[128]{0:T(128)S(1)}, f32[128]{0:T(128)}, u32[]{:S(2)}) %copy-start.2) | copy-done | bytes 536
  2.6 0.0 copy-start
  2.6 0.8 %copy-done = f32[128,128]{1,0:T(8,128)S(1)} copy-done((f32[128,128]{1,0:T(8,128)S(1)}, f32[128,128]{1,0:T(8,128)}, u32[]{:S(2)}) %copy-start) | copy-done | bytes 65560
  3.4 0.0 copy-start.1
  3.4 0.7 %copy-done.1 = f32[32,128]{1,0:T(8,128)S(1)} copy-done((f32[32,128]{1,0:T(8,128)S(1)}, f32[32,128]{1,0:T(8,128)}, u32[]{:S(2)}) %copy-start.1) | copy-done | bytes 16408
  4.1 35.1 %shard_map.68 = (f32[32,128]{1,0:T(8,128)S(1)}, f32[32,128]{1,0:T(8,128)S(1)}) custom-call(f32[128,128]{1,0:T(8,128)S(1)} %copy-done, f32[32,128]{1,0:T(8,128)S(1)} %copy-done.1, f32[1,128]{1,0:T(1,128)S(1)} %bitcast.1, f32[1]{0:T(128)S(6)} %copy.9.scale_ref, f32[1]{0:T(128)S(6)} %copy.10.noise_ref), custom_call_target="tpu_custom_call" | custom-call | tf_op jit(solution)/shard_map/pallas_call | solution.py:371
  39.2 0.6 %copy.11 = f32[32,128]{1,0:T(8,128)} copy(f32[32,128]{1,0:T(8,128)S(1)} %get-tuple-element.4) | data formatting | bytes 32768
  39.8 0.6 %copy.12 = f32[32,128]{1,0:T(8,128)} copy(f32[32,128]{1,0:T(8,128)S(1)} %get-tuple-element.5) | data formatting | bytes 32768
Async XLA Ops:
  1.9 0.7 %copy-start.2 = (f32[128]{0:T(128)S(1)}, f32[128]{0:T(128)}, u32[]{:S(2)}) copy-start(f32[128]{0:T(128)} %param.7) | copy-start | bytes 1540
  2.6 0.8 %copy-start = (f32[128,128]{1,0:T(8,128)S(1)}, f32[128,128]{1,0:T(8,128)}, u32[]{:S(2)}) copy-start(f32[128,128]{1,0:T(8,128)} %points_ref.1) | copy-start | bytes 196612
  3.4 0.7 %copy-start.1 = (f32[32,128]{1,0:T(8,128)S(1)}, f32[32,128]{1,0:T(8,128)}, u32[]{:S(2)}) copy-start(f32[32,128]{1,0:T(8,128)} %targets_ref.1) | copy-start | bytes 49156

commit v4 on v3

--- a/solution.py
+++ b/solution.py
@@ -168,13 +168,21 @@
 
 def fused(
     depth,
-    points_ref, targets_ref, lengths_ref, scale_ref, noise_ref,
+    points_hbm, targets_hbm, lengths_hbm, scale_ref, noise_ref,
     solution_ref, residual_ref,
     stack, images, kern_high, kern_low, parts, landing, scalars,
+    points_ref, targets_ref, lengths_ref, load_sem,
     send_a, recv_a, send_b, recv_b, send_p, recv_p, send_s, recv_s,
 ):
     features, local = points_ref.shape
     rhs = targets_ref.shape[0]
+    pairs = ((points_hbm, points_ref), (targets_hbm, targets_ref), (lengths_hbm, lengths_ref))
+    loads = [
+        pltpu.make_async_copy(source, target, load_sem.at[at])
+        for at, (source, target) in enumerate(pairs)
+    ]
+    for load in loads:
+        load.start()
     wide, row = lax.axis_index("wide"), lax.axis_index("row")
     core = lax.rem(wide, CORES)
     x = lax.rem(lax.div(wide, CORES), SIDE)
@@ -195,6 +203,8 @@
     for peer in everyone:
         pl.semaphore_signal(barrier, inc=1, device_id=place(*peer), device_id_type=MESH)
 
+    for load in loads:
+        load.wait()
     lengths = jnp.broadcast_to(lengths_ref[...], (features, features)).T
     targets = targets_ref[...]
     stack[0, :features, :] = points_ref[...] / lengths[:, :local]
@@ -364,6 +374,7 @@
     devices = lax.axis_size("wide") * lax.axis_size("row")
     depth = lax.axis_size("wide") // (CORES * SIDE)
     vmem, smem = pl.BlockSpec(memory_space=pltpu.VMEM), pl.BlockSpec(memory_space=pltpu.SMEM)
+    hbm = pl.BlockSpec(memory_space=pltpu.HBM)
     own = jax.ShapeDtypeStruct((rhs, local), jnp.float32)
     width = SIDE * SIDE * CORES
     near = width + depth - 1
@@ -371,7 +382,7 @@
     return pl.pallas_call(
         functools.partial(fused, depth),
         out_shape=(own, own),
-        in_specs=[vmem, vmem, vmem, smem, smem],
+        in_specs=[hbm, hbm, hbm, smem, smem],
         out_specs=(vmem, vmem),
         scratch_shapes=[
             pltpu.VMEM((near, features + rhs, local), jnp.float32),
@@ -380,7 +391,11 @@
             pltpu.VMEM((depth * width, local, local), jnp.bfloat16),
             pltpu.VMEM((2 * depth, rhs, local), jnp.float32),
             pltpu.VMEM((2 * depth, rhs, local), jnp.float32),
-            pltpu.VMEM((2 * devices, 8, local), jnp.float32),
+            pltpu.VMEM((2 * devices, 1, local), jnp.float32),
+            pltpu.VMEM((features, local), jnp.float32),
+            pltpu.VMEM((rhs, local), jnp.float32),
+            pltpu.VMEM((1, features), jnp.float32),
+            dma((3,)),
             dma((near,)),
             dma((near,)),
             dma((near,)),

time: 40.7 us -> 38.7 us (0.951)
  Pallas kernels: 35.1 us -> 33.1 us
    pallas_call x1, Pallas kernels: 35.1 us -> 33.1 us  [on_device_fused(): pl.pallas_call(functools.partial(fused, depth), out_shape=(own, own), in_...]
where the time goes in v4:
time: 38.7 us; the launch traced here: 38.5 us
  Pallas kernels  33.1 us (86%)
  local copies, waits for them, and re-layouts  3.42 us (9%)
  between operations  1.94 us (5%)
    pallas_call x1, Pallas kernels, on_device_fused(): pl.pallas_call(functools.partial(fused, depth), out_shape=(own, own), in_...  33.1 us
    unnamed x8, local copies, waits for them, and re-layouts  3.42 us

profile of v4, /device:TPU:0, one launch (start us, length us, event | category | flops | bytes accessed | tf_op | source)
XLA Modules:
  0.0 38.5 jit_solution(11009985313682677611)
XLA Ops:
  1.9 0.0 copy-start.2
  1.9 0.6 %copy-done.2 = f32[128]{0:T(128)S(1)} copy-done((f32[128]{0:T(128)S(1)}, f32[128]{0:T(128)}, u32[]{:S(2)}) %copy-start.2) | copy-done | bytes 536
  2.6 0.0 copy-start
  2.6 0.8 %copy-done = f32[128,128]{1,0:T(8,128)S(1)} copy-done((f32[128,128]{1,0:T(8,128)S(1)}, f32[128,128]{1,0:T(8,128)}, u32[]{:S(2)}) %copy-start) | copy-done | bytes 65560
  3.4 0.0 copy-start.1
  3.4 0.7 %copy-done.1 = f32[32,128]{1,0:T(8,128)S(1)} copy-done((f32[32,128]{1,0:T(8,128)S(1)}, f32[32,128]{1,0:T(8,128)}, u32[]{:S(2)}) %copy-start.1) | copy-done | bytes 16408
  4.1 33.1 %shard_map.68 = (f32[32,128]{1,0:T(8,128)S(1)}, f32[32,128]{1,0:T(8,128)S(1)}) custom-call(f32[128,128]{1,0:T(8,128)S(1)} %copy-done, f32[32,128]{1,0:T(8,128)S(1)} %copy-done.1, f32[1,128]{1,0:T(1,128)S(1)} %bitcast.1, f32[1]{0:T(128)S(6)} %copy.9.scale_ref, f32[1]{0:T(128)S(6)} %copy.10.noise_ref), custom_call_target="tpu_custom_call" | custom-call | tf_op jit(solution)/shard_map/pallas_call | solution.py:382
  37.3 0.6 %copy.11 = f32[32,128]{1,0:T(8,128)} copy(f32[32,128]{1,0:T(8,128)S(1)} %get-tuple-element.4) | data formatting | bytes 32768
  37.9 0.6 %copy.12 = f32[32,128]{1,0:T(8,128)} copy(f32[32,128]{1,0:T(8,128)S(1)} %get-tuple-element.5) | data formatting | bytes 32768
Async XLA Ops:
  1.9 0.7 %copy-start.2 = (f32[128]{0:T(128)S(1)}, f32[128]{0:T(128)}, u32[]{:S(2)}) copy-start(f32[128]{0:T(128)} %param.7) | copy-start | bytes 1540
  2.6 0.8 %copy-start = (f32[128,128]{1,0:T(8,128)S(1)}, f32[128,128]{1,0:T(8,128)}, u32[]{:S(2)}) copy-start(f32[128,128]{1,0:T(8,128)} %points_hbm.1) | copy-start | bytes 196612
  3.4 0.7 %copy-start.1 = (f32[32,128]{1,0:T(8,128)S(1)}, f32[32,128]{1,0:T(8,128)}, u32[]{:S(2)}) copy-start(f32[32,128]{1,0:T(8,128)} %targets_hbm.1) | copy-start | bytes 49156

commit v5 on v4

--- a/solution.py
+++ b/solution.py
@@ -330,8 +330,13 @@
     first_image = mine + noise_var * targets
     images[0] = first_image
     column, beside = spread(images, send_b, recv_b)
+    for to in across:
+        far = (to[0], to[1], 1)
+        at = number(*far)
+        beside[far] = copy(images.at[0], images.at[at], send_b, at, recv_b, at, (0, *far))
     sent = send_scalars(0, [targets * targets, targets * first_image, first_image * first_image])
-    relay(images, send_b, recv_b, beside)
+    for at in plane[1:]:
+        beside[at].wait_recv()
     for level in range(1, depth):
         column[level].wait_recv()
     found = all_scalars(0, sent)

time: 38.7 us -> 38.7 us (level)
  no operation moved by 1% of the time
where the time goes in v5:
time: 38.7 us; the launch traced here: 38.5 us
  Pallas kernels  33.1 us (86%)
  local copies, waits for them, and re-layouts  3.42 us (9%)
  between operations  1.94 us (5%)
    pallas_call x1, Pallas kernels, on_device_fused(): pl.pallas_call(functools.partial(fused, depth), out_shape=(own, own), in_...  33.1 us
    unnamed x8, local copies, waits for them, and re-layouts  3.42 us

profile of v5, /device:TPU:0, one launch (start us, length us, event | category | flops | bytes accessed | tf_op | source)
XLA Modules:
  0.0 38.5 jit_solution(8864434136255604901)
XLA Ops:
  1.9 0.0 copy-start.2
  1.9 0.6 %copy-done.2 = f32[128]{0:T(128)S(1)} copy-done((f32[128]{0:T(128)S(1)}, f32[128]{0:T(128)}, u32[]{:S(2)}) %copy-start.2) | copy-done | bytes 536
  2.6 0.0 copy-start
  2.6 0.8 %copy-done = f32[128,128]{1,0:T(8,128)S(1)} copy-done((f32[128,128]{1,0:T(8,128)S(1)}, f32[128,128]{1,0:T(8,128)}, u32[]{:S(2)}) %copy-start) | copy-done | bytes 65560
  3.4 0.0 copy-start.1
  3.4 0.7 %copy-done.1 = f32[32,128]{1,0:T(8,128)S(1)} copy-done((f32[32,128]{1,0:T(8,128)S(1)}, f32[32,128]{1,0:T(8,128)}, u32[]{:S(2)}) %copy-start.1) | copy-done | bytes 16408
  4.1 33.1 %shard_map.68 = (f32[32,128]{1,0:T(8,128)S(1)}, f32[32,128]{1,0:T(8,128)S(1)}) custom-call(f32[128,128]{1,0:T(8,128)S(1)} %copy-done, f32[32,128]{1,0:T(8,128)S(1)} %copy-done.1, f32[1,128]{1,0:T(1,128)S(1)} %bitcast.1, f32[1]{0:T(128)S(6)} %copy.9.scale_ref, f32[1]{0:T(128)S(6)} %copy.10.noise_ref), custom_call_target="tpu_custom_call" | custom-call | tf_op jit(solution)/shard_map/pallas_call | solution.py:387
  37.3 0.6 %copy.11 = f32[32,128]{1,0:T(8,128)} copy(f32[32,128]{1,0:T(8,128)S(1)} %get-tuple-element.4) | data formatting | bytes 32768
  37.9 0.6 %copy.12 = f32[32,128]{1,0:T(8,128)} copy(f32[32,128]{1,0:T(8,128)S(1)} %get-tuple-element.5) | data formatting | bytes 32768
Async XLA Ops:
  1.9 0.7 %copy-start.2 = (f32[128]{0:T(128)S(1)}, f32[128]{0:T(128)}, u32[]{:S(2)}) copy-start(f32[128]{0:T(128)} %param.7) | copy-start | bytes 1540
  2.6 0.8 %copy-start = (f32[128,128]{1,0:T(8,128)S(1)}, f32[128,128]{1,0:T(8,128)}, u32[]{:S(2)}) copy-start(f32[128,128]{1,0:T(8,128)} %points_hbm.1) | copy-start | bytes 196612
  3.4 0.7 %copy-start.1 = (f32[32,128]{1,0:T(8,128)S(1)}, f32[32,128]{1,0:T(8,128)}, u32[]{:S(2)}) copy-start(f32[32,128]{1,0:T(8,128)} %targets_hbm.1) | copy-start | bytes 49156
